TPU v7x, 512 devices: a whole 4x4x16 slice. The times are simulated.
512 devices in a mesh: ctx: 64 (over z, y), grp: 8 (over x, core).
Axes of the slice: x: 4, y: 4, z: 16, core: 2. Of those that a mesh axis runs over, the one named last changes fastest.
Arguments:
- query_nope: bfloat16 [64, 128, 128], P('grp', 'ctx'), parts along dimension 0, may hold values from -6 to 6
- query_rope: bfloat16 [64, 128, 64], P('grp', 'ctx'), parts along dimension 0, may hold values from -20 to 20
- weight_key: bfloat16 [128, 128, 512], P('ctx'), may hold values from -0.5 to 0.5
- weight_value: bfloat16 [128, 512, 128], P('ctx'), may hold values from -0.25 to 0.25
- cache_codes: bfloat16 [64, 24576, 512], P('grp', 'ctx'), parts along dimension 0, may hold values from -6 to 6
- cache_rope: bfloat16 [64, 24576, 64], P('grp', 'ctx'), parts along dimension 0, may hold values from -6 to 6
- cache_scale: float32 [64, 24576], P('grp', 'ctx'), parts along dimension 0, may hold values from 0.25 to 16, as said below
- lengths: int32 [64], P('grp'), parts along dimension 0, may hold values from 8192 to 24576
- tile_live: int32 [64, 192], P('grp', 'ctx'), parts along dimension 0, may hold values from 0 to 1, as said below
Outputs:
- attended: bfloat16 [64, 128, 128], P('grp', 'ctx'), parts along dimension 0
There are 8 independent parts, one for each index of `grp`. A program takes and returns all parts, laid end to end along the dimension named above; an argument that names none is the same for every part. Nothing has to cross between parts.
Inputs may be any that keep to these rules, and one draw needn't show every extreme that they name: `tile_live`: the first tile of every request is kept; tiles at or beyond a request's length are 0. `cache_scale`: positive scales.
All inputs are finite; a program needn't handle non-finite values.
Results may differ from a plain program's by a relative error of at most 0.012.
The roundings to bfloat16 on the way count: a program that leaves them out, or rounds other values in their place, can miss the bound.
Values may be sent and summed in bfloat16 or wider, within the bound.
A program may use at most 64 MiB of HBM per device.

v0:
```python
import jax
import jax.numpy as jnp
from jax import lax
from jax.sharding import PartitionSpec as P

score_factor = 0.0721688


def per_device(
    query_nope,
    query_rope,
    weight_key,
    weight_value,
    cache_codes,
    cache_rope,
    cache_scale,
    lengths,
    tile_live,
):
    query_latent = jnp.einsum(
        "bhn,hnl->bhl", query_nope, weight_key, preferred_element_type=jnp.float32
    ).astype(jnp.bfloat16)
    all_latent, all_rope = (
        lax.all_gather(query_latent, "ctx", axis=1, tiled=True),
        lax.all_gather(query_rope, "ctx", axis=1, tiled=True),
    )
    slots = cache_codes.shape[1]
    tile_size = slots // tile_live.shape[1]
    positions = lax.axis_index("ctx") * slots + jnp.arange(slots, dtype=jnp.int32)
    kept = jnp.repeat(tile_live, tile_size, axis=1) == 1
    valid = (positions[None, :] < lengths[:, None]) & kept
    part_latent = jnp.einsum(
        "bhl,bsl->bhs", all_latent, cache_codes, preferred_element_type=jnp.float32
    )
    part_rope = jnp.einsum("bhr,bsr->bhs", all_rope, cache_rope, preferred_element_type=jnp.float32)
    scores = score_factor * (cache_scale[:, None, :] * part_latent + part_rope)
    masked = jnp.where(valid[:, None, :], scores, jnp.float32(-1e30))
    local_top = jnp.max(masked, axis=2)
    top = lax.pmax(local_top, "ctx")
    expo = jnp.where(valid[:, None, :], jnp.exp(masked - top[:, :, None]), jnp.float32(0.0))
    total = jnp.sum(expo, axis=2)
    probs = (expo * cache_scale[:, None, :]).astype(jnp.bfloat16)
    summed = jnp.einsum("bhs,bsl->bhl", probs, cache_codes, preferred_element_type=jnp.float32)
    owned_sum, owned_total = (
        lax.psum_scatter(summed, "ctx", scatter_dimension=1, tiled=True),
        lax.psum_scatter(total, "ctx", scatter_dimension=1, tiled=True),
    )
    latent_out = (owned_sum / owned_total[:, :, None]).astype(jnp.bfloat16)
    attended = jnp.einsum(
        "bhl,hlv->bhv", latent_out, weight_value, preferred_element_type=jnp.float32
    )
    return attended.astype(jnp.bfloat16)


def solution(mesh):
    in_specs = (
        P("grp", "ctx", None),
        P("grp", "ctx", None),
        P("ctx", None, None),
        P("ctx", None, None),
        P("grp", "ctx", None),
        P("grp", "ctx", None),
        P("grp", "ctx"),
        P("grp"),
        P("grp", "ctx"),
    )
    out_specs = P("grp", "ctx", None)
    return jax.shard_map(
        per_device, mesh=mesh, in_specs=in_specs, out_specs=out_specs, check_vma=False
    )
```

profile of v0, /device:TPU:4, one launch (start us, length us, event | category | flops | bytes accessed | tf_op | source)
XLA Modules:
  0.0 999.3 jit_solution(4451008336549814336)
XLA Ops:
  6.5 0.0 copy-start
  6.5 0.0 all-gather.2.cloned.1.call-start
  6.5 1.8 fusion.1
  8.4 0.0 all-gather.2.cloned.1.call-update
  8.4 0.0 reduce-scatter.2.cloned.1.call-start
  8.5 0.7 copy.12
  9.2 89.0 %all_gather.7 = bf16[8,128,64]{2,0,1:T(8,128)(2,1)S(1)} all-gather(bf16[8,2,64]{2,0,1:T(8,128)(2,1)S(1)} %copy.12), channel_id=1, replica_groups=mesh['ctx'=64,'grp'=8] {'ctx'}, dimensions={1}, use_global_device_ids=true | all-gather | bytes 133120 | tf_op jit(solution)/shard_map/all_gather | solution.py:25
  98.2 0.7 broadcast_compare_fusion
  98.8 0.7 bitcast_and_fusion
  99.6 54.1 %all-gather.2.cloned.1.call-done = bf16[8,128,512]{2,0,1:T(8,128)(2,1)} async-done(((bf16[8,2,512]{2,0,1:T(8,128)(2,1)}), bf16[8,128,512]{2,0,1:T(8,128)(2,1)}) %all-gather.2.cloned.1.call-update) | async-done | bytes 1048592 | tf_op jit(solution)/shard_map/all_gather | solution.py:24
  153.7 0.0 copy-done
  153.7 2.4 fusion.3
  156.1 1.6 fusion.14
  157.7 141.6 %pmax.7 = f32[8,128]{1,0:T(8,128)S(1)} all-reduce(f32[8,128]{1,0:T(8,128)S(1)} %get-tuple-element.5), channel_id=1, replica_groups=mesh['ctx'=64,'grp'=8] {'ctx'}, use_global_device_ids=true, to_apply=%region_1.2 | all-reduce | flops 1024 | bytes 8192 | tf_op jit(solution)/shard_map/pmax | solution.py:39
  299.3 2.2 fusion.5
  301.5 2.6 copy.17
  304.1 0.0 reduce-scatter.2.cloned.1.call-update
  304.1 1.3 dynamic-slice
  306.1 1.9 fusion
  308.0 0.1 copy.14
  308.1 274.1 %all-reduce = f32[8,128]{0,1:T(8,128)S(1)} all-reduce(f32[8,128]{0,1:T(8,128)S(1)} %copy.14), channel_id=3, replica_groups=mesh['ctx'=64,'grp'=8] {'ctx'}, use_global_device_ids=true, to_apply=%region_4.5.clone | all-reduce | flops 1024 | bytes 8192
  582.1 408.8 %reduce-scatter.2.cloned.1.call-done = f32[8,2,512]{2,0,1:T(8,128)} async-done(((f32[8,128,512]{2,0,1:T(8,128)}), f32[8,2,512]{2,0,1:T(8,128)}) %reduce-scatter.2.cloned.1.call-update) | async-done | bytes 32784 | tf_op jit(solution)/shard_map/reduce_scatter | solution.py:45
  990.9 1.0 fusion.2
  991.9 0.6 copy.15
  (8 shorter events, 0.0 us)
Async XLA Ops:
  6.5 147.2 %copy-start = (bf16[8,384,512]{2,1,0:T(8,128)(2,1)S(1)}, bf16[8,384,512]{2,1,0:T(8,128)(2,1)}, u32[]{:S(2)}) copy-start(bf16[8,384,512]{2,1,0:T(8,128)(2,1)} %param.13) | copy-start | bytes 9437188
  6.5 147.2 %all-gather.2.cloned.1.call-start = ((), (), s32[]{:S(2)}) async-start(), calls=%async_computation.1 | async-start | bytes 1064960 | tf_op jit(solution)/shard_map/all_gather | solution.py:24
  8.4 982.5 %reduce-scatter.2.cloned.1.call-start = ((), (), s32[]{:S(2)}) async-start(), calls=%async_computation.2 | async-start | bytes 2129920 | tf_op jit(solution)/shard_map/reduce_scatter | solution.py:45
  99.6 56.5 %copy-start.3 = (f32[8,384]{1,0:T(8,128)S(1)}, f32[8,384]{1,0:T(8,128)}, u32[]{:S(2)}) copy-start(f32[8,384]{1,0:T(8,128)} %param.15) | copy-start | bytes 36868
  153.7 2.4 copy-start.1
  304.1 686.9 %copy-start.2 = (bf16[2,512,128]{2,1,0:T(8,128)(2,1)S(1)}, bf16[2,512,128]{2,1,0:T(8,128)(2,1)}, u32[]{:S(2)}) copy-start(bf16[2,512,128]{2,1,0:T(8,128)(2,1)} %param.12) | copy-start | bytes 786436
Sparse Core Ops, SparseCore 0:
  10.3 143.3 all-gather.1
  304.2 686.6 reduce-scatter.1
where the time goes:
time: 1000 us; the launch traced here: 999 us
  blocking collectives  505 us (50%)
  waiting for transfers between devices  463 us (46%)
  between operations  14.1 us (1%)
    reduce_scatter x1, waiting for transfers between devices, per_device(): lax.psum_scatter(summed, 'ctx', scatter_dimension=1, tiled=True)  409 us
    unnamed x1, blocking collectives  274 us
    pmax x1, blocking collectives, per_device(): top = lax.pmax(local_top, 'ctx')  142 us
    all_gather x1, blocking collectives, per_device(): lax.all_gather(query_rope, 'ctx', axis=1, tiled=True)  89 us
    all_gather x1, waiting for transfers between devices, per_device(): lax.all_gather(query_latent, 'ctx', axis=1, tiled=True)  54.1 us
  transfers between devices with their start and end apart: 2, of which 2 were waited for; matrix products, arithmetic and copies ran while one was open for 1% of the time, Pallas kernels for 0%

commit v1 on v0

v1 whole, which is shorter than its diff:
```python
import functools

import jax
import jax.numpy as jnp
from jax import lax
from jax.experimental import pallas as pl
from jax.experimental.pallas import tpu as pltpu
from jax.sharding import PartitionSpec as P

score_factor = 0.0721688
NZ, NY = 16, 4
B, DL, DR, DN, DV = 8, 512, 64, 128, 128
SLOTS, TILE = 384, 128
QW = 640
MESH = pl.DeviceIdType.MESH
Z_OFFS = (8, 7, -7, 6, -6, 5, -5, 4, -4, 3, -3, 2, -2, 1, -1)
Y_OFFS = (2, 1, -1)
f32 = jnp.float32
bf16 = jnp.bfloat16


def kernel(
    q_ref, wk_hbm, wv_hbm, codes_hbm, rope_hbm, scale_ref, len_ref, live_ref, out_ref,
    wk, wv, codes, rope, zbuf, zf, qbuf, obuf, rbuf, sbuf, srbuf, zr, zsend, zrecv, tsend, trecv,
    load_sem, zs, zrs, ys, yr, ps, pr, pss, psr, os_, or_, oss, osr,
):
    me = lax.axis_index("ctx")
    z, y = me // NY, lax.rem(me, NY)

    def zdev(k):
        return {"ctx": lax.rem(z + k + NZ, NZ) * NY + y}

    def ydev(k):
        return {"ctx": z * NY + lax.rem(y + k + NY, NY)}

    def load(i):
        if i == 0:
            return pltpu.make_async_copy(wk_hbm, wk, load_sem.at[0])
        if i == 1:
            return pltpu.make_async_copy(codes_hbm, codes, load_sem.at[1])
        if i == 2:
            return pltpu.make_async_copy(rope_hbm, rope, load_sem.at[2])
        return pltpu.make_async_copy(wv_hbm, wv, load_sem.at[3])

    for i in range(4):
        load(i).start()

    barrier = pltpu.get_barrier_semaphore()
    for k in Z_OFFS:
        pl.semaphore_signal(barrier, inc=1, device_id=zdev(k), device_id_type=MESH)
    for k in Y_OFFS:
        pl.semaphore_signal(barrier, inc=1, device_id=ydev(k), device_id_type=MESH)

    load(0).wait()
    latent = jnp.concatenate(
        [jnp.dot(q_ref[h, :, :DN], wk[h], preferred_element_type=f32) for h in range(2)], axis=0
    )
    zbuf[z, :, :DL] = latent.astype(bf16)
    zbuf[z, :, DL:] = jnp.concatenate([q_ref[h, :, DN:].astype(f32) for h in range(2)], axis=0).astype(bf16)

    pl.semaphore_wait(barrier, len(Z_OFFS) + len(Y_OFFS))

    def zcopy(i):
        return pltpu.make_async_remote_copy(
            zbuf.at[z], zbuf.at[z], zs.at[i], zrs.at[i], device_id=zdev(Z_OFFS[i]), device_id_type=MESH
        )

    for i in range(len(Z_OFFS)):
        zcopy(i).start()
    for i in range(len(Z_OFFS)):
        zcopy(i).wait_recv()
    for s in range(NZ):
        for j in range(QW // 128):
            zf[j, pl.ds(s * 16, 16), :] = zbuf[s, :, j * 128 : (j + 1) * 128].astype(f32)

    def ycopy(b, i):
        return pltpu.make_async_remote_copy(
            qbuf.at[b, y], qbuf.at[b, y], ys.at[b, i], yr.at[b, i],
            device_id=ydev(Y_OFFS[i]), device_id_type=MESH,
        )

    def spread(b, c):
        for j in range(QW // 128):
            qbuf[b, y, :, pl.ds(j * 128, 128)] = zf[j, pl.ds(b, 32, stride=8), :].astype(bf16)
        for i in range(3):
            ycopy(b, i).start()
        return c

    lax.fori_loop(0, B, spread, 0)
    load(1).wait()
    load(2).wait()

    def pcopy(b, i):
        return pltpu.make_async_remote_copy(
            obuf.at[b, lax.rem(y + Y_OFFS[i] + NY, NY)], rbuf.at[b, i], ps.at[b, i], pr.at[b, i],
            device_id=ydev(Y_OFFS[i]), device_id_type=MESH,
        )

    def scopy(b, i):
        return pltpu.make_async_remote_copy(
            sbuf.at[b], srbuf.at[b, i], pss.at[b, i], psr.at[b, i],
            device_id=ydev(Y_OFFS[i]), device_id_type=MESH,
        )

    lane = lax.broadcasted_iota(jnp.int32, (1, TILE), 1)
    heads = NY * 32
    eye = lax.broadcasted_iota(jnp.int32, (heads, heads), 0) == lax.broadcasted_iota(
        jnp.int32, (heads, heads), 1
    )

    def attend(b, c):
        for i in range(3):
            ycopy(b, i).wait_recv()
        q = qbuf[b].reshape(heads, QW)
        nt = (((1,), (1,)), ((), ()))
        codes_b = codes[b]
        part = lax.dot_general(q[:, :DL], codes_b, nt, preferred_element_type=f32)
        turned = lax.dot_general(q[:, DL : DL + DR], rope[b], nt, preferred_element_type=f32)
        scale = scale_ref[pl.ds(b, 1), :]
        length = len_ref[b]
        flags = []
        for t in range(SLOTS // TILE):
            limit = jnp.where(live_ref[b, t] == 1, length - (me * SLOTS + t * TILE), 0)
            flags.append(jnp.where(lane < limit, f32(1.0), f32(0.0)))
        valid = jnp.concatenate(flags, axis=1) > 0.5
        scores = score_factor * (scale * part + turned)
        masked = jnp.where(valid, scores, f32(-1e30))
        top = jnp.max(masked, axis=1, keepdims=True)
        expo = jnp.where(valid, jnp.exp(masked - top), f32(0.0))
        total = jnp.sum(expo, axis=1, keepdims=True)
        probs = (expo * scale).astype(bf16)
        summed = jnp.dot(probs, codes_b, preferred_element_type=f32)
        obuf[b] = summed.astype(bf16).reshape(NY, 32, DL)
        sbuf[b, pl.ds(0, 1), :] = jnp.sum(jnp.where(eye, top, f32(0.0)), axis=0, keepdims=True)
        sbuf[b, pl.ds(1, 1), :] = jnp.sum(jnp.where(eye, total, f32(0.0)), axis=0, keepdims=True)
        for i in range(3):
            pcopy(b, i).start()
            scopy(b, i).start()
        return c

    lax.fori_loop(0, B, attend, 0)

    rows32 = lax.broadcasted_iota(jnp.int32, (32, 128), 0)
    lanes32 = lax.broadcasted_iota(jnp.int32, (32, 128), 1)
    pick = lanes32 == rows32 + y * 32

    def column(row):
        return jnp.sum(jnp.where(pick, row, f32(0.0)), axis=1, keepdims=True)

    def combine(b, stats):
        for i in range(3):
            pcopy(b, i).wait_recv()
            scopy(b, i).wait_recv()
        tops = [column(sbuf[b, pl.ds(0, 1), :])] + [column(srbuf[b, i, pl.ds(0, 1), :]) for i in range(3)]
        totals = [column(sbuf[b, pl.ds(1, 1), :])] + [column(srbuf[b, i, pl.ds(1, 1), :]) for i in range(3)]
        top = functools.reduce(jnp.maximum, tops)
        factors = [jnp.exp(t - top) for t in tops]
        total = sum(f * t for f, t in zip(factors, totals))
        summed = factors[0] * obuf[b, y].astype(f32)
        for i in range(3):
            summed = summed + factors[i + 1] * rbuf[b, i].astype(f32)
        for j in range(DL // 128):
            zr[j, pl.ds(b, 32, stride=8), :] = summed[:, j * 128 : (j + 1) * 128]
        stats = jnp.where(lanes32 == b, top, stats)
        return jnp.where(lanes32 == B + b, total, stats)

    stats = lax.fori_loop(0, B, combine, jnp.zeros((32, 128), f32))
    for s in range(NZ):
        for j in range(DL // 128):
            zsend[s, :, j * 128 : (j + 1) * 128] = zr[j, pl.ds(s * 16, 16), :].astype(bf16)
        tsend[s] = stats[s * 2 : s * 2 + 2, :]

    def ocopy(i):
        k = Z_OFFS[i]
        return pltpu.make_async_remote_copy(
            zsend.at[lax.rem(z + k + NZ, NZ)], zrecv.at[i], os_.at[i], or_.at[i],
            device_id=zdev(k), device_id_type=MESH,
        )

    def tcopy(i):
        k = Z_OFFS[i]
        return pltpu.make_async_remote_copy(
            tsend.at[lax.rem(z + k + NZ, NZ)], trecv.at[i], oss.at[i], osr.at[i],
            device_id=zdev(k), device_id_type=MESH,
        )

    for i in range(len(Z_OFFS)):
        ocopy(i).start()
        tcopy(i).start()

    rows16 = lax.broadcasted_iota(jnp.int32, (8, 128), 0)
    lanes16 = lax.broadcasted_iota(jnp.int32, (8, 128), 1)

    def column16(two, first):
        return jnp.concatenate(
            [
                jnp.sum(jnp.where(lanes16 == rows16 + first, two[h : h + 1, :], f32(0.0)), axis=1, keepdims=True)
                for h in range(2)
            ],
            axis=0,
        )

    load(3).wait()
    for i in range(len(Z_OFFS)):
        tcopy(i).wait_recv()
    pairs = [tsend[z]] + [trecv[i] for i in range(len(Z_OFFS))]
    tops = [column16(p, 0) for p in pairs]
    totals = [column16(p, B) for p in pairs]
    top = functools.reduce(jnp.maximum, tops)
    factors = [jnp.exp(t - top) for t in tops]
    total = sum(f * t for f, t in zip(factors, totals))
    for i in range(len(Z_OFFS)):
        ocopy(i).wait_recv()
    summed = factors[0] * zsend[z].astype(f32)
    for i in range(len(Z_OFFS)):
        summed = summed + factors[i + 1] * zrecv[i].astype(f32)
    latent_out = (summed / total).astype(bf16)
    for h in range(2):
        out_ref[h] = jnp.dot(
            latent_out[h * 8 : h * 8 + 8, :], wv[h], preferred_element_type=f32
        ).astype(bf16)

    for i in range(len(Z_OFFS)):
        zcopy(i).wait_send()
        ocopy(i).wait_send()
        tcopy(i).wait_send()

    def drain(b, c):
        for i in range(3):
            ycopy(b, i).wait_send()
            pcopy(b, i).wait_send()
            scopy(b, i).wait_send()
        return c

    lax.fori_loop(0, B, drain, 0)


def per_device(
    query_nope, query_rope, weight_key, weight_value, cache_codes, cache_rope, cache_scale, lengths, tile_live
):
    pad = jnp.zeros((B, 2, 64), bf16)
    query = jnp.concatenate([query_nope, query_rope, pad], axis=2).transpose(1, 0, 2)
    hbm = pl.BlockSpec(memory_space=pl.ANY)
    vmem = pl.BlockSpec(memory_space=pltpu.VMEM)
    smem = pl.BlockSpec(memory_space=pltpu.SMEM)
    dma = pltpu.SemaphoreType.DMA
    n = len(Z_OFFS)
    out = pl.pallas_call(
        kernel,
        out_shape=jax.ShapeDtypeStruct((2, B, DV), bf16),
        in_specs=[vmem, hbm, hbm, hbm, hbm, vmem, smem, smem],
        out_specs=vmem,
        scratch_shapes=[
            pltpu.VMEM((2, DN, DL), bf16),
            pltpu.VMEM((2, DL, DV), bf16),
            pltpu.VMEM((B, SLOTS, DL), bf16),
            pltpu.VMEM((B, SLOTS, DR), bf16),
            pltpu.VMEM((NZ, 16, QW), bf16),
            pltpu.VMEM((QW // 128, NZ * 16, 128), f32),
            pltpu.VMEM((B, NY, 32, QW), bf16),
            pltpu.VMEM((B, NY, 32, DL), bf16),
            pltpu.VMEM((B, 3, 32, DL), bf16),
            pltpu.VMEM((B, 2, 128), f32),
            pltpu.VMEM((B, 3, 2, 128), f32),
            pltpu.VMEM((DL // 128, NZ * 16, 128), f32),
            pltpu.VMEM((NZ, 16, DL), bf16),
            pltpu.VMEM((n, 16, DL), bf16),
            pltpu.VMEM((NZ, 2, 128), f32),
            pltpu.VMEM((n, 2, 128), f32),
            dma((4,)),
            dma((n,)), dma((n,)),
            dma((B, 3)), dma((B, 3)),
            dma((B, 3)), dma((B, 3)),
            dma((B, 3)), dma((B, 3)),
            dma((n,)), dma((n,)),
            dma((n,)), dma((n,)),
        ],
        compiler_params=pltpu.CompilerParams(
            collective_id=0, has_side_effects=True, vmem_limit_bytes=40 * 1024 * 1024
        ),
        cost_estimate=pl.CostEstimate(flops=860_000_000, bytes_accessed=4_500_000, transcendentals=400_000),
        name="latent_decode",
    )(query, weight_key, weight_value, cache_codes, cache_rope, cache_scale, lengths, tile_live)
    return out.transpose(1, 0, 2)


def solution(mesh):
    in_specs = (
        P("grp", "ctx", None),
        P("grp", "ctx", None),
        P("ctx", None, None),
        P("ctx", None, None),
        P("grp", "ctx", None),
        P("grp", "ctx", None),
        P("grp", "ctx"),
        P("grp"),
        P("grp", "ctx"),
    )
    return jax.shard_map(
        per_device, mesh=mesh, in_specs=in_specs, out_specs=P("grp", "ctx", None), check_vma=False
    )
```

time: 1000 us -> 86.9 us (0.09)
  the two profiles are of different devices: /device:TPU:4 before, /device:TPU:1 now
where the time goes in v1:
time: 86.9 us; the launch traced here: 86.5 us
  Pallas kernels  77.2 us (89%)
  local copies, waits for them, and re-layouts  9.33 us (11%)
    pallas_call x1, Pallas kernels, per_device(): pl.pallas_call(kernel, out_shape=jax.ShapeDtypeStruct((2, B, DV), bf16),...  77.2 us
    unnamed x14, local copies, waits for them, and re-layouts  8.65 us

profile of v1, /device:TPU:1, one launch (start us, length us, event | category | flops | bytes accessed | tf_op | source)
XLA Modules:
  0.0 86.5 jit_solution(13039747235885614895)
XLA Ops:
  0.0 0.1 pad.2.clone
  0.1 0.7 copy.10
  0.8 0.7 copy.11
  1.5 0.8 copy.13.live_ref
  2.2 1.4 %copy.12.rope_hbm = bf16[8,384,64]{2,1,0:T(8,128)(2,1)S(1)} copy(bf16[8,384,64]{1,2,0:T(8,128)(2,1)} %param.14) | data formatting | bytes 786432 | tf_op args[5]
  3.6 0.0 copy-start
  3.6 1.9 %copy-done = bf16[8,384,512]{2,1,0:T(8,128)(2,1)S(1)} copy-done((bf16[8,384,512]{2,1,0:T(8,128)(2,1)S(1)}, bf16[8,384,512]{2,1,0:T(8,128)(2,1)}, u32[]{:S(2)}) %copy-start) | copy-done | bytes 3145752
  5.5 0.0 copy-start.1
  5.5 0.9 %copy-done.1 = bf16[2,128,512]{2,1,0:T(8,128)(2,1)S(1)} copy-done((bf16[2,128,512]{2,1,0:T(8,128)(2,1)S(1)}, bf16[2,128,512]{2,1,0:T(8,128)(2,1)}, u32[]{:S(2)}) %copy-start.1) | copy-done | bytes 262168
  6.4 0.0 copy-start.2
  6.5 0.9 %copy-done.2 = bf16[2,512,128]{2,1,0:T(8,128)(2,1)S(1)} copy-done((bf16[2,512,128]{2,1,0:T(8,128)(2,1)S(1)}, bf16[2,512,128]{2,1,0:T(8,128)(2,1)}, u32[]{:S(2)}) %copy-start.2) | copy-done | bytes 262168
  7.4 0.0 copy-start.3
  7.4 0.7 copy-done.3
  8.1 0.0 copy-start.4
  8.1 0.7 copy-done.4
  8.8 77.2 %latent_decode.1 = bf16[2,8,128]{2,1,0:T(8,128)(2,1)S(1)} custom-call(bf16[2,8,256]{2,1,0:T(8,128)(2,1)S(1)} %maximum_bitcast_fusion.q_ref, bf16[2,128,512]{2,1,0:T(8,128)(2,1)S(1)} %copy-done.1, bf16[2,512,128]{2,1,0:T(8,128)(2,1)S(1)} %copy-done.2, bf16[8,384,512]{2,1,0:T(8,128)(2,1)S(1)} %copy-done, bf16[8,384,64]{2,1,0:T(8,128)(2,1)S(1)} %copy.12.rope_hbm, ...), custom_call_target="tpu_custom_call" | custom-call | flops 860000000 | bytes 4500000 | tf_op jit(solution)/shard_map/latent_decode/pallas_call | solution.py:248
  85.9 0.6 copy.14
  (2 shorter events, 0.0 us)
Async XLA Ops:
  3.6 1.9 %copy-start = (bf16[8,384,512]{2,1,0:T(8,128)(2,1)S(1)}, bf16[8,384,512]{2,1,0:T(8,128)(2,1)}, u32[]{:S(2)}) copy-start(bf16[8,384,512]{2,1,0:T(8,128)(2,1)} %codes_hbm.1) | copy-start | bytes 9437188
  5.5 0.9 %copy-start.1 = (bf16[2,128,512]{2,1,0:T(8,128)(2,1)S(1)}, bf16[2,128,512]{2,1,0:T(8,128)(2,1)}, u32[]{:S(2)}) copy-start(bf16[2,128,512]{2,1,0:T(8,128)(2,1)} %wk_hbm.1) | copy-start | bytes 786436
  6.4 0.9 %copy-start.2 = (bf16[2,512,128]{2,1,0:T(8,128)(2,1)S(1)}, bf16[2,512,128]{2,1,0:T(8,128)(2,1)}, u32[]{:S(2)}) copy-start(bf16[2,512,128]{2,1,0:T(8,128)(2,1)} %wv_hbm.1) | copy-start | bytes 786436
  7.4 0.7 copy-start.3
  8.1 0.7 copy-start.4

commit v2 on v0

v2 whole, which is shorter than its diff:
```python
import functools

import jax
import jax.numpy as jnp
from jax import lax
from jax.experimental import pallas as pl
from jax.experimental.pallas import tpu as pltpu
from jax.sharding import PartitionSpec as P

score_factor = 0.0721688
NZ, NY = 16, 4
B, DL, DR, DN, DV = 8, 512, 64, 128, 128
SLOTS, TILE = 384, 128
NC = 4
BC = B // NC
ROWS = 2 * B
PART = DL // NC
QW = DL + 128
HEADS = NY * 2 * NZ
MESH = pl.DeviceIdType.MESH
FAR = (0, 4, -4, 8)
NEAR = (0, 2, 1, -1)
SLOT_OFFS = tuple((f + n + 7) % NZ - 7 for f in FAR for n in NEAR)
ORDER = tuple(sorted(range(1, NZ), key=lambda s: -abs(SLOT_OFFS[s])))
Y_OFFS = (2, 1, -1)
f32 = jnp.float32
bf16 = jnp.bfloat16


def kernel(
    qn_hbm, qr_hbm, wk_hbm, wv_hbm, codes_hbm, rope_hbm, scale_hbm, len_hbm, live_hbm, out_ref,
    qn, qr, wk, wv, codes, rope, scales, lens, live,
    qall, zf, obuf, rbuf, sbuf, srbuf, zr, zsend, zrecv, tsend, trecv,
    load_sem, fs, fr, ns, nr, ys, yr, hs, hr, ps, pr, pss, psr, os_, or_, oss, osr,
):
    me = lax.axis_index("ctx")
    z, y = me // NY, lax.rem(me, NY)

    def zid(k):
        return lax.rem(z + k + NZ, NZ)

    def yid(k):
        return lax.rem(y + k + NY, NY)

    def zdev(k):
        return {"ctx": zid(k) * NY + y}

    def ydev(k):
        return {"ctx": z * NY + yid(k)}

    def remote(src, dst, send, recv, device):
        return pltpu.make_async_remote_copy(
            src, dst, send, recv, device_id=device, device_id_type=MESH
        )

    pairs = (
        (qn_hbm, qn), (qr_hbm, qr), (wk_hbm, wk), (codes_hbm, codes), (rope_hbm, rope),
        (scale_hbm, scales), (len_hbm, lens), (live_hbm, live), (wv_hbm, wv),
    )

    def load(i):
        return pltpu.make_async_copy(pairs[i][0], pairs[i][1], load_sem.at[i])

    for i in range(len(pairs)):
        load(i).start()

    barrier = pltpu.get_barrier_semaphore()
    for k in SLOT_OFFS[1:]:
        pl.semaphore_signal(barrier, inc=1, device_id=zdev(k), device_id_type=MESH)
    for k in Y_OFFS:
        pl.semaphore_signal(barrier, inc=1, device_id=ydev(k), device_id_type=MESH)

    for i in range(3):
        load(i).wait()
    odd = lax.rem(lax.broadcasted_iota(jnp.int32, (ROWS, DL), 0), 2) == 1
    latent = jnp.where(
        odd,
        jnp.dot(qn[...], wk[1], preferred_element_type=f32),
        jnp.dot(qn[...], wk[0], preferred_element_type=f32),
    )
    qall[y, 0, 0, :, :DL] = latent.astype(bf16)
    qall[y, 0, 0, :, DL:] = jnp.concatenate(
        [qr[...].astype(f32), jnp.zeros((ROWS, 128 - DR), f32)], axis=1
    ).astype(bf16)

    pl.semaphore_wait(barrier, NZ - 1 + len(Y_OFFS))

    def far(f):
        return remote(qall.at[y, 0, 0], qall.at[y, f, 0], fs.at[f], fr.at[f], zdev(FAR[f]))

    def near(f, n):
        return remote(qall.at[y, f, 0], qall.at[y, f, n], ns.at[f, n], nr.at[f, n], zdev(NEAR[n]))

    def ycopy(f, i):
        mine = qall.at[y, f]
        return remote(mine, mine, ys.at[f, i], yr.at[f, i], ydev((1, -1)[i]))

    def hand(f, i):
        block = qall.at[yid((-1, 1)[i]), f, pl.ds((2, 0)[i], 2)]
        return remote(block, block, hs.at[f, i], hr.at[f, i], ydev((1, -1)[i]))

    def near_start(f):
        for n in range(1, 4):
            near(f, n).start()

    def y_start(f):
        for n in range(1, 4):
            near(f, n).wait_recv()
        for i in range(2):
            ycopy(f, i).start()

    def hand_start(f):
        for i in range(2):
            ycopy(f, i).wait_recv()
            hand(f, i).start()

    def widen(f):
        for i in range(2):
            hand(f, i).wait_recv()

        def store(v, carry):
            for n in range(4):
                block = qall[v, f, n].astype(f32)
                for j in range(QW // 128):
                    start = pl.multiple_of((v * NZ + f * 4 + n) * ROWS, ROWS)
                    zf[j, pl.ds(start, ROWS), :] = block[:, j * 128 : (j + 1) * 128]
            return carry

        lax.fori_loop(0, NY, store, 0)

    for f in (3, 1, 2):
        far(f).start()
    near_start(0)
    y_start(0)
    far(1).wait_recv()
    near_start(1)
    far(2).wait_recv()
    near_start(2)
    hand_start(0)
    far(3).wait_recv()
    near_start(3)
    y_start(1)
    y_start(2)
    hand_start(1)
    y_start(3)
    widen(0)
    hand_start(2)
    widen(1)
    hand_start(3)
    widen(2)
    for i in range(3, 8):
        load(i).wait()
    widen(3)

    def pcopy(c, i):
        return remote(
            obuf.at[c, yid(Y_OFFS[i])], rbuf.at[c, i], ps.at[c, i], pr.at[c, i], ydev(Y_OFFS[i])
        )

    def scopy(c, i):
        return remote(sbuf.at[c], srbuf.at[c, i], pss.at[c, i], psr.at[c, i], ydev(Y_OFFS[i]))

    lane = lax.broadcasted_iota(jnp.int32, (1, TILE), 1)
    eye = lax.broadcasted_iota(jnp.int32, (HEADS, HEADS), 0) == lax.broadcasted_iota(
        jnp.int32, (HEADS, HEADS), 1
    )

    def attend_one(c, r, carry):
        b = c * BC + r
        q = jnp.concatenate(
            [
                jnp.concatenate(
                    [
                        zf[j, pl.ds(v * NZ * ROWS + b * 2 + h, NZ, stride=ROWS), :].astype(bf16)
                        for v in range(NY)
                        for h in range(2)
                    ],
                    axis=0,
                )
                for j in range(QW // 128)
            ],
            axis=1,
        )
        codes_b = codes[b]
        part = lax.dot_general(
            q[:, :DL], codes_b, (((1,), (1,)), ((), ())), preferred_element_type=f32
        )
        turned = jnp.dot(q[:, DL : DL + DR], rope[b], preferred_element_type=f32)
        scale = scales[pl.ds(b, 1), :]
        length = lens[b]
        flags = []
        for t in range(SLOTS // TILE):
            limit = jnp.where(live[t, b] == 1, length - (me * SLOTS + t * TILE), 0)
            flags.append(jnp.where(lane < limit, f32(1.0), f32(0.0)))
        valid = jnp.concatenate(flags, axis=1) > 0.5
        scores = score_factor * (scale * part + turned)
        masked = jnp.where(valid, scores, f32(-1e30))
        top = jnp.max(masked, axis=1, keepdims=True)
        expo = jnp.where(valid, jnp.exp(masked - top), f32(0.0))
        total = jnp.sum(expo, axis=1, keepdims=True)
        probs = (expo * scale).astype(bf16)
        summed = jnp.dot(probs, codes_b, preferred_element_type=f32)
        for v in range(NY):
            obuf[c, v, r] = summed[v * 32 : v * 32 + 32].astype(bf16)
        sbuf[c, r, pl.ds(0, 1), :] = jnp.sum(jnp.where(eye, top, f32(0.0)), axis=0, keepdims=True)
        sbuf[c, r, pl.ds(1, 1), :] = jnp.sum(jnp.where(eye, total, f32(0.0)), axis=0, keepdims=True)
        return carry

    def attend(c):
        lax.fori_loop(0, BC, functools.partial(attend_one, c), 0)

    def pass_on(c):
        for i in range(3):
            scopy(c, i).start()
            pcopy(c, i).start()

    rows32 = lax.broadcasted_iota(jnp.int32, (32, 128), 0)
    lanes32 = lax.broadcasted_iota(jnp.int32, (32, 128), 1)
    pick = lanes32 == rows32 + y * 32
    lanes16 = lax.broadcasted_iota(jnp.int32, (NZ, 128), 1)

    def column(row):
        return jnp.sum(jnp.where(pick, row, f32(0.0)), axis=1, keepdims=True)

    def combine_one(c, r, stats):
        rows = [sbuf[c, r]] + [srbuf[c, i, r] for i in range(3)]
        tops = [column(t[0:1]) for t in rows]
        totals = [column(t[1:2]) for t in rows]
        top = functools.reduce(jnp.maximum, tops)
        factors = [jnp.exp(t - top) for t in tops]
        total = sum(f * t for f, t in zip(factors, totals))
        summed = factors[0] * obuf[c, y, r].astype(f32)
        for i in range(3):
            summed = summed + factors[i + 1] * rbuf[c, i, r].astype(f32)
        first, second = stats
        for h in range(2):
            mine = slice(h * 16, h * 16 + 16)
            for k in range(NC):
                for j in range(PART // 128):
                    lanes = k * PART + j * 128
                    zr[j, pl.ds(k * 2 * BC + r * 2 + h, 16, stride=16), :] = summed[mine, lanes : lanes + 128]
            first = jnp.where(lanes16 == (c * BC + r) * 2 + h, top[mine], first)
            second = jnp.where(lanes16 == (c * BC + r) * 2 + h, total[mine], second)
        return first, second

    def ocopy(c, s):
        return remote(zsend.at[c, s], zrecv.at[c, s], os_.at[c, s], or_.at[c, s], zdev(-SLOT_OFFS[s]))

    def tcopy(s):
        return remote(tsend.at[s], trecv.at[s], oss.at[s], osr.at[s], zdev(-SLOT_OFFS[s]))

    def combine(c, stats):
        for i in range(3):
            scopy(c, i).wait_recv()
            pcopy(c, i).wait_recv()
        stats = lax.fori_loop(0, BC, functools.partial(combine_one, c), stats)
        for s in range(NZ):
            for j in range(PART // 128):
                zsend[c, s, :, j * 128 : (j + 1) * 128] = zr[j, pl.ds(s * 16, 16), :].astype(bf16)
        for i in ORDER:
            ocopy(c, i).start()
        return stats

    def attend_all(c, carry):
        attend(c)
        pass_on(c)
        return carry

    lax.fori_loop(0, NC, attend_all, 0)
    blank = jnp.zeros((NZ, 128), f32)
    stats = lax.fori_loop(0, NC, combine, (blank, blank))
    for s in range(NZ):
        for p in range(2):
            tsend[s, p : p + 1, :] = stats[p][s : s + 1]
    for i in ORDER:
        tcopy(i).start()

    load(8).wait()
    odd16 = lax.rem(lax.broadcasted_iota(jnp.int32, (ROWS, DV), 0), 2) == 1
    for i in ORDER:
        tcopy(i).wait_recv()
    both = [tsend[0]] + [trecv[i] for i in range(1, NZ)]
    tops = jnp.concatenate([t[0:1] for t in both], axis=0)
    totals = jnp.concatenate([t[1:2] for t in both], axis=0)
    weights = jnp.exp(tops - jnp.max(tops, axis=0, keepdims=True))
    whole = jnp.sum(weights * totals, axis=0, keepdims=True)
    finished = []
    for c in range(NC):
        spot = lanes16 == c * 2 * BC + lax.rem(lax.broadcasted_iota(jnp.int32, (ROWS, 128), 0), 2 * BC)

        def spread_out(row, spot=spot):
            return jnp.sum(jnp.where(spot, row, f32(0.0)), axis=1, keepdims=True)

        summed = spread_out(weights[0:1]) * zsend[c, 0].astype(f32)
        for i in range(1, NZ):
            ocopy(c, i).wait_recv()
            summed = summed + spread_out(weights[i : i + 1]) * zrecv[c, i].astype(f32)
        summed = summed / spread_out(whole)
        finished.append(jnp.concatenate([summed[k * 2 * BC : (k + 1) * 2 * BC] for k in range(NC)], axis=1))
    latent_out = jnp.concatenate(finished, axis=0).astype(bf16)
    out_ref[...] = jnp.where(
        odd16,
        jnp.dot(latent_out, wv[1], preferred_element_type=f32),
        jnp.dot(latent_out, wv[0], preferred_element_type=f32),
    ).astype(bf16)

    for f in range(4):
        if f:
            far(f).wait_send()
        for n in range(1, 4):
            near(f, n).wait_send()
        for i in range(2):
            ycopy(f, i).wait_send()
            hand(f, i).wait_send()
    for i in ORDER:
        tcopy(i).wait_send()

    def drain(c, carry):
        for i in range(3):
            pcopy(c, i).wait_send()
            scopy(c, i).wait_send()
        for i in ORDER:
            ocopy(c, i).wait_send()
        return carry

    lax.fori_loop(0, NC, drain, 0)


def per_device(
    query_nope, query_rope, weight_key, weight_value, cache_codes, cache_rope, cache_scale, lengths, tile_live
):
    hbm = pl.BlockSpec(memory_space=pl.ANY)
    dma = pltpu.SemaphoreType.DMA
    vmem = pltpu.VMEM
    out = pl.pallas_call(
        kernel,
        out_shape=jax.ShapeDtypeStruct((ROWS, DV), bf16),
        in_specs=[hbm] * 9,
        out_specs=pl.BlockSpec(memory_space=pltpu.VMEM),
        scratch_shapes=[
            vmem((ROWS, DN), bf16),
            vmem((ROWS, DR), bf16),
            vmem((2, DN, DL), bf16),
            vmem((2, DL, DV), bf16),
            vmem((B, SLOTS, DL), bf16),
            vmem((B, DR, SLOTS), bf16),
            vmem((B, SLOTS), f32),
            pltpu.SMEM((B,), jnp.int32),
            pltpu.SMEM((SLOTS // TILE, B), jnp.int32),
            vmem((NY, 4, 4, ROWS, QW), bf16),
            vmem((QW // 128, NY * NZ * ROWS, 128), f32),
            vmem((NC, NY, BC, 32, DL), bf16),
            vmem((NC, 3, BC, 32, DL), bf16),
            vmem((NC, BC, 2, 128), f32),
            vmem((NC, 3, BC, 2, 128), f32),
            vmem((PART // 128, NZ * 16, 128), f32),
            vmem((NC, NZ, 16, PART), bf16),
            vmem((NC, NZ, 16, PART), bf16),
            vmem((NZ, 2, 128), f32),
            vmem((NZ, 2, 128), f32),
            dma((9,)),
            dma((4,)), dma((4,)),
            dma((4, 4)), dma((4, 4)),
            dma((4, 2)), dma((4, 2)),
            dma((4, 2)), dma((4, 2)),
            dma((NC, 3)), dma((NC, 3)),
            dma((NC, 3)), dma((NC, 3)),
            dma((NC, NZ)), dma((NC, NZ)),
            dma((NZ,)), dma((NZ,)),
        ],
        compiler_params=pltpu.CompilerParams(
            collective_id=0, has_side_effects=True, vmem_limit_bytes=60 * 1024 * 1024
        ),
        cost_estimate=pl.CostEstimate(flops=860_000_000, bytes_accessed=4_500_000, transcendentals=400_000),
        name="latent_decode",
    )(
        query_nope.reshape(ROWS, DN), query_rope.reshape(ROWS, DR), weight_key, weight_value, cache_codes,
        cache_rope.swapaxes(1, 2), cache_scale, lengths, tile_live.T,
    )
    return out.reshape(B, 2, DV)


def solution(mesh):
    in_specs = (
        P("grp", "ctx", None),
        P("grp", "ctx", None),
        P("ctx", None, None),
        P("ctx", None, None),
        P("grp", "ctx", None),
        P("grp", "ctx", None),
        P("grp", "ctx"),
        P("grp"),
        P("grp", "ctx"),
    )
    return jax.shard_map(
        per_device, mesh=mesh, in_specs=in_specs, out_specs=P("grp", "ctx", None), check_vma=False
    )
```

time: 1000 us -> 69 us (0.07)
  the two profiles are of different devices: /device:TPU:4 before, /device:TPU:2 now
where the time goes in v2:
time: 69 us; the launch traced here: 68.8 us
  Pallas kernels  67.5 us (98%)
  local copies, waits for them, and re-layouts  1.28 us (2%)
    pallas_call x1, Pallas kernels, per_device(): pl.pallas_call(kernel, out_shape=jax.ShapeDtypeStruct((ROWS, DV), bf16),...  67.5 us

profile of v2, /device:TPU:2, one launch (start us, length us, event | category | flops | bytes accessed | tf_op | source)
XLA Modules:
  0.0 68.8 jit_solution(16512342936507121813)
XLA Ops:
  0.0 67.5 %latent_decode.1 = bf16[16,128]{1,0:T(8,128)(2,1)} custom-call(bf16[16,128]{1,0:T(8,128)(2,1)} %bitcast.7, bf16[16,64]{1,0:T(8,128)(2,1)} %bitcast.8, bf16[2,128,512]{2,1,0:T(8,128)(2,1)} %wk_hbm.1, bf16[2,512,128]{2,1,0:T(8,128)(2,1)} %wv_hbm.1, bf16[8,384,512]{2,1,0:T(8,128)(2,1)} %codes_hbm.1, bf16[8,64,384]{2,1,0:T(8,128)(2,1)} %bitcast.5, ...), custom_call_target="tpu_custom_call" | custom-call | flops 860000000 | bytes 4500000 | tf_op jit(solution)/shard_map/latent_decode/pallas_call | solution.py:335
  67.5 1.3 %copy.11 = bf16[8,2,128]{2,1,0:T(2,128)(2,1)} copy(bf16[8,2,128]{2,1,0:T(2,128)(2,1)} %bitcast.6) | data formatting | bytes 8192

commit v3 on v2

--- a/solution.py
+++ b/solution.py
@@ -18,10 +18,18 @@
 QW = DL + 128
 HEADS = NY * 2 * NZ
 MESH = pl.DeviceIdType.MESH
-FAR = (0, 4, -4, 8)
-NEAR = (0, 2, 1, -1)
-SLOT_OFFS = tuple((f + n + 7) % NZ - 7 for f in FAR for n in NEAR)
-ORDER = tuple(sorted(range(1, NZ), key=lambda s: -abs(SLOT_OFFS[s])))
+FAR = (0, 5, -5)
+NEAR = (0, 1, -1, 2, -2, 3)
+SIZE = (5, 6, 5)
+FIRST = (0, 5, 11)
+SLOT_PATHS = tuple((f, n) for f in range(3) for n in range(SIZE[f]))
+Z_PARTNERS = (5, -5, 3, -3, 2, -2, 1, -1)
+
+
+def place(f, n):
+    return 3 * n + f if n < 5 else 15
+
+
 Y_OFFS = (2, 1, -1)
 f32 = jnp.float32
 bf16 = jnp.bfloat16
@@ -30,8 +38,8 @@
 def kernel(
     qn_hbm, qr_hbm, wk_hbm, wv_hbm, codes_hbm, rope_hbm, scale_hbm, len_hbm, live_hbm, out_ref,
     qn, qr, wk, wv, codes, rope, scales, lens, live,
-    qall, zf, obuf, rbuf, sbuf, srbuf, zr, zsend, zrecv, tsend, trecv,
-    load_sem, fs, fr, ns, nr, ys, yr, hs, hr, ps, pr, pss, psr, os_, or_, oss, osr,
+    qall, zf, obuf, rbuf, sbuf, srbuf, zr, zsend, zrecv, tsend, trecv, mown, msend, mrecv, mtsend, mtrecv,
+    load_sem, fs, fr, ns, nr, ys, yr, hs, hr, ps, pr, pss, psr, os_, or_, oss, osr, ms, mr, mss, msr,
 ):
     me = lax.axis_index("ctx")
     z, y = me // NY, lax.rem(me, NY)
@@ -65,7 +73,7 @@
         load(i).start()
 
     barrier = pltpu.get_barrier_semaphore()
-    for k in SLOT_OFFS[1:]:
+    for k in Z_PARTNERS:
         pl.semaphore_signal(barrier, inc=1, device_id=zdev(k), device_id_type=MESH)
     for k in Y_OFFS:
         pl.semaphore_signal(barrier, inc=1, device_id=ydev(k), device_id_type=MESH)
@@ -78,33 +86,35 @@
         jnp.dot(qn[...], wk[1], preferred_element_type=f32),
         jnp.dot(qn[...], wk[0], preferred_element_type=f32),
     )
-    qall[y, 0, 0, :, :DL] = latent.astype(bf16)
-    qall[y, 0, 0, :, DL:] = jnp.concatenate(
+    qall[y, 0, :, :DL] = latent.astype(bf16)
+    qall[y, 0, :, DL:] = jnp.concatenate(
         [qr[...].astype(f32), jnp.zeros((ROWS, 128 - DR), f32)], axis=1
     ).astype(bf16)
 
-    pl.semaphore_wait(barrier, NZ - 1 + len(Y_OFFS))
+    pl.semaphore_wait(barrier, len(Z_PARTNERS) + len(Y_OFFS))
 
     def far(f):
-        return remote(qall.at[y, 0, 0], qall.at[y, f, 0], fs.at[f], fr.at[f], zdev(FAR[f]))
+        return remote(qall.at[y, 0], qall.at[y, FIRST[f]], fs.at[f], fr.at[f], zdev(FAR[f]))
 
     def near(f, n):
-        return remote(qall.at[y, f, 0], qall.at[y, f, n], ns.at[f, n], nr.at[f, n], zdev(NEAR[n]))
+        s = FIRST[f] + n
+        return remote(qall.at[y, FIRST[f]], qall.at[y, s], ns.at[s], nr.at[s], zdev(NEAR[n]))
 
     def ycopy(f, i):
-        mine = qall.at[y, f]
+        mine = qall.at[y, pl.ds(FIRST[f], SIZE[f])]
         return remote(mine, mine, ys.at[f, i], yr.at[f, i], ydev((1, -1)[i]))
 
     def hand(f, i):
-        block = qall.at[yid((-1, 1)[i]), f, pl.ds((2, 0)[i], 2)]
+        part = (pl.ds(FIRST[f] + 3, SIZE[f] - 3), pl.ds(FIRST[f], 3))[i]
+        block = qall.at[yid((-1, 1)[i]), part]
         return remote(block, block, hs.at[f, i], hr.at[f, i], ydev((1, -1)[i]))
 
     def near_start(f):
-        for n in range(1, 4):
+        for n in range(SIZE[f] - 1, 0, -1):
             near(f, n).start()
 
     def y_start(f):
-        for n in range(1, 4):
+        for n in range(1, SIZE[f]):
             near(f, n).wait_recv()
         for i in range(2):
             ycopy(f, i).start()
@@ -119,17 +129,17 @@
             hand(f, i).wait_recv()
 
         def store(v, carry):
-            for n in range(4):
-                block = qall[v, f, n].astype(f32)
+            for n in range(SIZE[f]):
+                block = qall[v, FIRST[f] + n].astype(f32)
                 for j in range(QW // 128):
-                    start = pl.multiple_of((v * NZ + f * 4 + n) * ROWS, ROWS)
+                    start = pl.multiple_of((v * NZ + FIRST[f] + n) * ROWS, ROWS)
                     zf[j, pl.ds(start, ROWS), :] = block[:, j * 128 : (j + 1) * 128]
             return carry
 
         lax.fori_loop(0, NY, store, 0)
 
-    for f in (3, 1, 2):
-        far(f).start()
+    far(1).start()
+    far(2).start()
     near_start(0)
     y_start(0)
     far(1).wait_recv()
@@ -137,20 +147,15 @@
     far(2).wait_recv()
     near_start(2)
     hand_start(0)
-    far(3).wait_recv()
-    near_start(3)
     y_start(1)
     y_start(2)
+    widen(0)
     hand_start(1)
-    y_start(3)
-    widen(0)
     hand_start(2)
-    widen(1)
-    hand_start(3)
-    widen(2)
     for i in range(3, 8):
         load(i).wait()
-    widen(3)
+    widen(1)
+    widen(2)
 
     def pcopy(c, i):
         return remote(
@@ -236,30 +241,75 @@
         for h in range(2):
             mine = slice(h * 16, h * 16 + 16)
             for k in range(NC):
-                for j in range(PART // 128):
-                    lanes = k * PART + j * 128
-                    zr[j, pl.ds(k * 2 * BC + r * 2 + h, 16, stride=16), :] = summed[mine, lanes : lanes + 128]
-            first = jnp.where(lanes16 == (c * BC + r) * 2 + h, top[mine], first)
-            second = jnp.where(lanes16 == (c * BC + r) * 2 + h, total[mine], second)
+                zr[pl.ds(k * 2 * BC + r * 2 + h, 16, stride=16), :] = summed[mine, k * PART : (k + 1) * PART]
+            first = jnp.where(lanes16 == r * 2 + h, top[mine], first)
+            second = jnp.where(lanes16 == r * 2 + h, total[mine], second)
         return first, second
 
-    def ocopy(c, s):
-        return remote(zsend.at[c, s], zrecv.at[c, s], os_.at[c, s], or_.at[c, s], zdev(-SLOT_OFFS[s]))
-
-    def tcopy(s):
-        return remote(tsend.at[s], trecv.at[s], oss.at[s], osr.at[s], zdev(-SLOT_OFFS[s]))
-
-    def combine(c, stats):
+    def group(n):
+        return pl.ds(3 * n, 3) if n < 5 else pl.ds(15, 1)
+
+    def ocopy(c, n):
+        part = group(n)
+        return remote(zsend.at[c, part], zrecv.at[c, part], os_.at[c, n], or_.at[c, n], zdev(-NEAR[n]))
+
+    def tcopy(c, n):
+        part = group(n)
+        return remote(tsend.at[c, part], trecv.at[c, part], oss.at[c, n], osr.at[c, n], zdev(-NEAR[n]))
+
+    def mcopy(c, f):
+        return remote(msend.at[c, f], mrecv.at[c, f], ms.at[c, f], mr.at[c, f], zdev(-FAR[f]))
+
+    def mtcopy(c, f):
+        return remote(mtsend.at[c, f], mtrecv.at[c, f], mss.at[c, f], msr.at[c, f], zdev(-FAR[f]))
+
+    def combine(c, carry):
         for i in range(3):
             scopy(c, i).wait_recv()
             pcopy(c, i).wait_recv()
-        stats = lax.fori_loop(0, BC, functools.partial(combine_one, c), stats)
-        for s in range(NZ):
-            for j in range(PART // 128):
-                zsend[c, s, :, j * 128 : (j + 1) * 128] = zr[j, pl.ds(s * 16, 16), :].astype(bf16)
-        for i in ORDER:
-            ocopy(c, i).start()
-        return stats
+        blank = jnp.zeros((NZ, 128), f32)
+        first, second = lax.fori_loop(0, BC, functools.partial(combine_one, c), (blank, blank))
+        for s, path in enumerate(SLOT_PATHS):
+            p = place(*path)
+            zsend[c, p] = zr[pl.ds(s * 16, 16), :].astype(bf16)
+            tsend[c, p, 0:1, :] = first[s : s + 1]
+            tsend[c, p, 1:2, :] = second[s : s + 1]
+        for n in range(5, 0, -1):
+            tcopy(c, n).start()
+            ocopy(c, n).start()
+        return carry
+
+    spot = lanes16 == lax.rem(lax.broadcasted_iota(jnp.int32, (ROWS, 128), 0), 2 * BC)
+
+    def spread_out(row):
+        return jnp.sum(jnp.where(spot, row, f32(0.0)), axis=1, keepdims=True)
+
+    def merge(stats, blocks):
+        tops = [t[0:1] for t in stats]
+        top = functools.reduce(jnp.maximum, tops)
+        weights = [jnp.exp(t - top) for t in tops]
+        whole = sum(w * t[1:2] for w, t in zip(weights, stats))
+        return top, whole, sum(spread_out(w) * block.astype(f32) for w, block in zip(weights, blocks))
+
+    def middle(c, carry):
+        for n in range(1, 6):
+            tcopy(c, n).wait_recv()
+            ocopy(c, n).wait_recv()
+        for f in (1, 2, 0):
+            places = [place(f, n) for n in range(1, SIZE[f])]
+            top, whole, summed = merge(
+                [tsend[c, f]] + [trecv[c, p] for p in places],
+                [zsend[c, f]] + [zrecv[c, p] for p in places],
+            )
+            mtsend[c, f, 0:1, :] = top
+            mtsend[c, f, 1:2, :] = whole
+            if f == 0:
+                mown[c] = summed
+            else:
+                msend[c, f] = summed.astype(bf16)
+                mtcopy(c, f).start()
+                mcopy(c, f).start()
+        return carry
 
     def attend_all(c, carry):
         attend(c)
@@ -267,36 +317,23 @@
         return carry
 
     lax.fori_loop(0, NC, attend_all, 0)
-    blank = jnp.zeros((NZ, 128), f32)
-    stats = lax.fori_loop(0, NC, combine, (blank, blank))
-    for s in range(NZ):
-        for p in range(2):
-            tsend[s, p : p + 1, :] = stats[p][s : s + 1]
-    for i in ORDER:
-        tcopy(i).start()
+    lax.fori_loop(0, NC, combine, 0)
+    lax.fori_loop(0, NC, middle, 0)
 
     load(8).wait()
     odd16 = lax.rem(lax.broadcasted_iota(jnp.int32, (ROWS, DV), 0), 2) == 1
-    for i in ORDER:
-        tcopy(i).wait_recv()
-    both = [tsend[0]] + [trecv[i] for i in range(1, NZ)]
-    tops = jnp.concatenate([t[0:1] for t in both], axis=0)
-    totals = jnp.concatenate([t[1:2] for t in both], axis=0)
-    weights = jnp.exp(tops - jnp.max(tops, axis=0, keepdims=True))
-    whole = jnp.sum(weights * totals, axis=0, keepdims=True)
     finished = []
     for c in range(NC):
-        spot = lanes16 == c * 2 * BC + lax.rem(lax.broadcasted_iota(jnp.int32, (ROWS, 128), 0), 2 * BC)
-
-        def spread_out(row, spot=spot):
-            return jnp.sum(jnp.where(spot, row, f32(0.0)), axis=1, keepdims=True)
-
-        summed = spread_out(weights[0:1]) * zsend[c, 0].astype(f32)
-        for i in range(1, NZ):
-            ocopy(c, i).wait_recv()
-            summed = summed + spread_out(weights[i : i + 1]) * zrecv[c, i].astype(f32)
+        for f in (1, 2):
+            mtcopy(c, f).wait_recv()
+            mcopy(c, f).wait_recv()
+        _, whole, summed = merge(
+            [mtsend[c, 0], mtrecv[c, 1], mtrecv[c, 2]], [mown[c], mrecv[c, 1], mrecv[c, 2]]
+        )
         summed = summed / spread_out(whole)
-        finished.append(jnp.concatenate([summed[k * 2 * BC : (k + 1) * 2 * BC] for k in range(NC)], axis=1))
+        finished.append(
+            jnp.concatenate([summed[k * 2 * BC : (k + 1) * 2 * BC] for k in range(NC)], axis=1)
+        )
     latent_out = jnp.concatenate(finished, axis=0).astype(bf16)
     out_ref[...] = jnp.where(
         odd16,
@@ -304,23 +341,25 @@
         jnp.dot(latent_out, wv[0], preferred_element_type=f32),
     ).astype(bf16)
 
-    for f in range(4):
+    for f in range(3):
         if f:
             far(f).wait_send()
-        for n in range(1, 4):
+        for n in range(1, SIZE[f]):
             near(f, n).wait_send()
         for i in range(2):
             ycopy(f, i).wait_send()
             hand(f, i).wait_send()
-    for i in ORDER:
-        tcopy(i).wait_send()
 
     def drain(c, carry):
         for i in range(3):
             pcopy(c, i).wait_send()
             scopy(c, i).wait_send()
-        for i in ORDER:
-            ocopy(c, i).wait_send()
+        for n in range(1, 6):
+            tcopy(c, n).wait_send()
+            ocopy(c, n).wait_send()
+        for f in (1, 2):
+            mtcopy(c, f).wait_send()
+            mcopy(c, f).wait_send()
         return carry
 
     lax.fori_loop(0, NC, drain, 0)
@@ -347,26 +386,33 @@
             vmem((B, SLOTS), f32),
             pltpu.SMEM((B,), jnp.int32),
             pltpu.SMEM((SLOTS // TILE, B), jnp.int32),
-            vmem((NY, 4, 4, ROWS, QW), bf16),
+            vmem((NY, NZ, ROWS, QW), bf16),
             vmem((QW // 128, NY * NZ * ROWS, 128), f32),
             vmem((NC, NY, BC, 32, DL), bf16),
             vmem((NC, 3, BC, 32, DL), bf16),
             vmem((NC, BC, 2, 128), f32),
             vmem((NC, 3, BC, 2, 128), f32),
-            vmem((PART // 128, NZ * 16, 128), f32),
+            vmem((NZ * 16, PART), f32),
             vmem((NC, NZ, 16, PART), bf16),
             vmem((NC, NZ, 16, PART), bf16),
-            vmem((NZ, 2, 128), f32),
-            vmem((NZ, 2, 128), f32),
+            vmem((NC, NZ, 2, 128), f32),
+            vmem((NC, NZ, 2, 128), f32),
+            vmem((NC, 16, PART), f32),
+            vmem((NC, 3, 16, PART), bf16),
+            vmem((NC, 3, 16, PART), bf16),
+            vmem((NC, 3, 2, 128), f32),
+            vmem((NC, 3, 2, 128), f32),
             dma((9,)),
-            dma((4,)), dma((4,)),
-            dma((4, 4)), dma((4, 4)),
-            dma((4, 2)), dma((4, 2)),
-            dma((4, 2)), dma((4, 2)),
+            dma((3,)), dma((3,)),
+            dma((NZ,)), dma((NZ,)),
+            dma((3, 2)), dma((3, 2)),
+            dma((3, 2)), dma((3, 2)),
             dma((NC, 3)), dma((NC, 3)),
             dma((NC, 3)), dma((NC, 3)),
-            dma((NC, NZ)), dma((NC, NZ)),
-            dma((NZ,)), dma((NZ,)),
+            dma((NC, 6)), dma((NC, 6)),
+            dma((NC, 6)), dma((NC, 6)),
+            dma((NC, 3)), dma((NC, 3)),
+            dma((NC, 3)), dma((NC, 3)),
         ],
         compiler_params=pltpu.CompilerParams(
             collective_id=0, has_side_effects=True, vmem_limit_bytes=60 * 1024 * 1024

time: 69 us -> 61.3 us (0.89)
  the two profiles are of different devices: /device:TPU:2 before, /device:TPU:4 now
where the time goes in v3:
time: 61.3 us; the launch traced here: 61.1 us
  Pallas kernels  59.8 us (98%)
  local copies, waits for them, and re-layouts  1.28 us (2%)
    pallas_call x1, Pallas kernels, per_device(): pl.pallas_call(kernel, out_shape=jax.ShapeDtypeStruct((ROWS, DV), bf16),...  59.8 us
    unnamed x1, local copies, waits for them, and re-layouts  1.28 us

profile of v3, /device:TPU:4, one launch (start us, length us, event | category | flops | bytes accessed | tf_op | source)
XLA Modules:
  0.0 61.1 jit_solution(12568980825922479548)
XLA Ops:
  0.0 59.8 %latent_decode.1 = bf16[16,128]{1,0:T(8,128)(2,1)} custom-call(bf16[16,128]{1,0:T(8,128)(2,1)} %bitcast.7, bf16[16,64]{1,0:T(8,128)(2,1)} %bitcast.8, bf16[2,128,512]{2,1,0:T(8,128)(2,1)} %wk_hbm.1, bf16[2,512,128]{2,1,0:T(8,128)(2,1)} %wv_hbm.1, bf16[8,384,512]{2,1,0:T(8,128)(2,1)} %codes_hbm.1, bf16[8,64,384]{2,1,0:T(8,128)(2,1)} %bitcast.5, ...), custom_call_target="tpu_custom_call" | custom-call | flops 860000000 | bytes 4500000 | tf_op jit(solution)/shard_map/latent_decode/pallas_call | solution.py:374
  59.8 1.3 %copy.11 = bf16[8,2,128]{2,1,0:T(2,128)(2,1)} copy(bf16[8,2,128]{2,1,0:T(2,128)(2,1)} %bitcast.6) | data formatting | bytes 8192

commit v4 on v3

--- a/solution.py
+++ b/solution.py
@@ -11,6 +11,7 @@
 NZ, NY = 16, 4
 B, DL, DR, DN, DV = 8, 512, 64, 128, 128
 SLOTS, TILE = 384, 128
+NB = 1
 NC = 4
 BC = B // NC
 ROWS = 2 * B
@@ -22,7 +23,8 @@
 NEAR = (0, 1, -1, 2, -2, 3)
 SIZE = (5, 6, 5)
 FIRST = (0, 5, 11)
-SLOT_PATHS = tuple((f, n) for f in range(3) for n in range(SIZE[f]))
+PIECES = ((0, 1), (1, 4), (5, 1), (6, 5), (11, 1), (12, 4))
+HANDED = 3
 Z_PARTNERS = (5, -5, 3, -3, 2, -2, 1, -1)
 
 
@@ -33,13 +35,17 @@
 Y_OFFS = (2, 1, -1)
 f32 = jnp.float32
 bf16 = jnp.bfloat16
+
+
+PLACES = tuple(place(f, n) for f in range(3) for n in range(SIZE[f]))
 
 
 def kernel(
     qn_hbm, qr_hbm, wk_hbm, wv_hbm, codes_hbm, rope_hbm, scale_hbm, len_hbm, live_hbm, out_ref,
     qn, qr, wk, wv, codes, rope, scales, lens, live,
     qall, zf, obuf, rbuf, sbuf, srbuf, zr, zsend, zrecv, tsend, trecv, mown, msend, mrecv, mtsend, mtrecv,
-    load_sem, fs, fr, ns, nr, ys, yr, hs, hr, ps, pr, pss, psr, os_, or_, oss, osr, ms, mr, mss, msr,
+    zb, bsend, brecv, tb, trb, ysend, yrecv, yt, ytr,
+    load_sem, fs, fr, ns, nr, ys, yr, hs, hr, ps, pr, pss, psr, os_, or_, oss, osr, ms, mr, mss, msr, bs, br, bts, btr, es, er, ets, etr,
 ):
     me = lax.axis_index("ctx")
     z, y = me // NY, lax.rem(me, NY)
@@ -100,39 +106,45 @@
         s = FIRST[f] + n
         return remote(qall.at[y, FIRST[f]], qall.at[y, s], ns.at[s], nr.at[s], zdev(NEAR[n]))
 
-    def ycopy(f, i):
-        mine = qall.at[y, pl.ds(FIRST[f], SIZE[f])]
-        return remote(mine, mine, ys.at[f, i], yr.at[f, i], ydev((1, -1)[i]))
-
-    def hand(f, i):
-        part = (pl.ds(FIRST[f] + 3, SIZE[f] - 3), pl.ds(FIRST[f], 3))[i]
+    def ycopy(p, i):
+        mine = qall.at[y, pl.ds(*PIECES[p])]
+        return remote(mine, mine, ys.at[p, i], yr.at[p, i], ydev((1, -1, 2)[i]))
+
+    def partners(p):
+        return range(2 if p == HANDED else 3)
+
+    def hand(i):
+        start, size = PIECES[HANDED]
+        part = (pl.ds(start + 3, size - 3), pl.ds(start, 3))[i]
         block = qall.at[yid((-1, 1)[i]), part]
-        return remote(block, block, hs.at[f, i], hr.at[f, i], ydev((1, -1)[i]))
+        return remote(block, block, hs.at[i], hr.at[i], ydev((1, -1)[i]))
 
     def near_start(f):
         for n in range(SIZE[f] - 1, 0, -1):
             near(f, n).start()
 
-    def y_start(f):
+    def near_wait(f):
         for n in range(1, SIZE[f]):
             near(f, n).wait_recv()
-        for i in range(2):
-            ycopy(f, i).start()
-
-    def hand_start(f):
-        for i in range(2):
-            ycopy(f, i).wait_recv()
-            hand(f, i).start()
-
-    def widen(f):
-        for i in range(2):
-            hand(f, i).wait_recv()
+
+    def y_start(p):
+        for i in partners(p):
+            ycopy(p, i).start()
+
+    def widen(p):
+        if p == HANDED:
+            for i in range(2):
+                hand(i).wait_recv()
+        else:
+            for i in range(3):
+                ycopy(p, i).wait_recv()
+        first, size = PIECES[p]
 
         def store(v, carry):
-            for n in range(SIZE[f]):
-                block = qall[v, FIRST[f] + n].astype(f32)
+            for n in range(size):
+                block = qall[v, first + n].astype(f32)
                 for j in range(QW // 128):
-                    start = pl.multiple_of((v * NZ + FIRST[f] + n) * ROWS, ROWS)
+                    start = pl.multiple_of((v * NZ + PLACES[first + n]) * ROWS, ROWS)
                     zf[j, pl.ds(start, ROWS), :] = block[:, j * 128 : (j + 1) * 128]
             return carry
 
@@ -142,35 +154,43 @@
     far(2).start()
     near_start(0)
     y_start(0)
+    near_wait(0)
+    y_start(1)
     far(1).wait_recv()
     near_start(1)
+    y_start(2)
     far(2).wait_recv()
     near_start(2)
-    hand_start(0)
-    y_start(1)
-    y_start(2)
-    widen(0)
-    hand_start(1)
-    hand_start(2)
+    y_start(4)
+    near_wait(1)
+    y_start(3)
+    near_wait(2)
+    y_start(5)
+    for p in (0, 1, 2, 4):
+        widen(p)
+    for i in range(2):
+        ycopy(HANDED, i).wait_recv()
+        hand(i).start()
     for i in range(3, 8):
         load(i).wait()
-    widen(1)
-    widen(2)
-
-    def pcopy(c, i):
+    widen(5)
+    widen(3)
+
+    def pcopy(c, r, i):
         return remote(
-            obuf.at[c, yid(Y_OFFS[i])], rbuf.at[c, i], ps.at[c, i], pr.at[c, i], ydev(Y_OFFS[i])
+            obuf.at[c, yid(Y_OFFS[i]), r], rbuf.at[c, i, r], ps.at[c, r, i], pr.at[c, r, i], ydev(Y_OFFS[i])
         )
 
     def scopy(c, i):
         return remote(sbuf.at[c], srbuf.at[c, i], pss.at[c, i], psr.at[c, i], ydev(Y_OFFS[i]))
 
     lane = lax.broadcasted_iota(jnp.int32, (1, TILE), 1)
+    lanes16 = lax.broadcasted_iota(jnp.int32, (NZ, 128), 1)
     eye = lax.broadcasted_iota(jnp.int32, (HEADS, HEADS), 0) == lax.broadcasted_iota(
         jnp.int32, (HEADS, HEADS), 1
     )
 
-    def attend_one(c, r, carry):
+    def attend_one(c, r):
         b = c * BC + r
         q = jnp.concatenate(
             [
@@ -205,24 +225,40 @@
         total = jnp.sum(expo, axis=1, keepdims=True)
         probs = (expo * scale).astype(bf16)
         summed = jnp.dot(probs, codes_b, preferred_element_type=f32)
+        return top, total, summed
+
+    def attend_y(c, r, carry):
+        top, total, summed = attend_one(c, r)
         for v in range(NY):
             obuf[c, v, r] = summed[v * 32 : v * 32 + 32].astype(bf16)
+        for i in range(3):
+            pcopy(c, r, i).start()
         sbuf[c, r, pl.ds(0, 1), :] = jnp.sum(jnp.where(eye, top, f32(0.0)), axis=0, keepdims=True)
         sbuf[c, r, pl.ds(1, 1), :] = jnp.sum(jnp.where(eye, total, f32(0.0)), axis=0, keepdims=True)
         return carry
 
-    def attend(c):
-        lax.fori_loop(0, BC, functools.partial(attend_one, c), 0)
+    def attend_z(c, r, stats):
+        found = attend_one(c, r)
+        for v in range(NY):
+            for h in range(2):
+                mine = slice(v * 32 + h * 16, v * 32 + h * 16 + 16)
+                for k in range(NC):
+                    zb[pl.ds(v * 256 + k * 2 * BC + r * 2 + h, 16, stride=16), :] = found[2][
+                        mine, k * PART : (k + 1) * PART
+                    ]
+                stats = tuple(
+                    jnp.where(lanes16 == r * 2 + h, found[i % 2][mine], old) if i // 2 == v else old
+                    for i, old in enumerate(stats)
+                )
+        return stats
 
     def pass_on(c):
         for i in range(3):
             scopy(c, i).start()
-            pcopy(c, i).start()
 
     rows32 = lax.broadcasted_iota(jnp.int32, (32, 128), 0)
     lanes32 = lax.broadcasted_iota(jnp.int32, (32, 128), 1)
     pick = lanes32 == rows32 + y * 32
-    lanes16 = lax.broadcasted_iota(jnp.int32, (NZ, 128), 1)
 
     def column(row):
         return jnp.sum(jnp.where(pick, row, f32(0.0)), axis=1, keepdims=True)
@@ -266,14 +302,14 @@
     def combine(c, carry):
         for i in range(3):
             scopy(c, i).wait_recv()
-            pcopy(c, i).wait_recv()
+            for r in range(BC):
+                pcopy(c, r, i).wait_recv()
         blank = jnp.zeros((NZ, 128), f32)
         first, second = lax.fori_loop(0, BC, functools.partial(combine_one, c), (blank, blank))
-        for s, path in enumerate(SLOT_PATHS):
-            p = place(*path)
-            zsend[c, p] = zr[pl.ds(s * 16, 16), :].astype(bf16)
-            tsend[c, p, 0:1, :] = first[s : s + 1]
-            tsend[c, p, 1:2, :] = second[s : s + 1]
+        for p in range(NZ):
+            zsend[c, p] = zr[pl.ds(p * 16, 16), :].astype(bf16)
+            tsend[c, p, 0:1, :] = first[p : p + 1]
+            tsend[c, p, 1:2, :] = second[p : p + 1]
         for n in range(5, 0, -1):
             tcopy(c, n).start()
             ocopy(c, n).start()
@@ -284,12 +320,27 @@
     def spread_out(row):
         return jnp.sum(jnp.where(spot, row, f32(0.0)), axis=1, keepdims=True)
 
-    def merge(stats, blocks):
-        tops = [t[0:1] for t in stats]
+    def merge_rows(own, others, blocks):
+        tops = [own[0]] + [t[0] for t in others]
+        totals = [own[1]] + [t[1] for t in others]
         top = functools.reduce(jnp.maximum, tops)
         weights = [jnp.exp(t - top) for t in tops]
-        whole = sum(w * t[1:2] for w, t in zip(weights, stats))
+        whole = sum(w * t for w, t in zip(weights, totals))
         return top, whole, sum(spread_out(w) * block.astype(f32) for w, block in zip(weights, blocks))
+
+    def merge(stats, blocks):
+        rows = [(t[0:1], t[1:2]) for t in stats]
+        return merge_rows(rows[0], rows[1:], blocks)
+
+    def forward(c, f, top, whole, summed):
+        mtsend[c, f, 0:1, :] = top
+        mtsend[c, f, 1:2, :] = whole
+        if f == 0:
+            mown[c] = summed
+        else:
+            msend[c, f] = summed.astype(bf16)
+            mtcopy(c, f).start()
+            mcopy(c, f).start()
 
     def middle(c, carry):
         for n in range(1, 6):
@@ -297,28 +348,94 @@
             ocopy(c, n).wait_recv()
         for f in (1, 2, 0):
             places = [place(f, n) for n in range(1, SIZE[f])]
-            top, whole, summed = merge(
+            merged = merge(
                 [tsend[c, f]] + [trecv[c, p] for p in places],
                 [zsend[c, f]] + [zrecv[c, p] for p in places],
             )
-            mtsend[c, f, 0:1, :] = top
-            mtsend[c, f, 1:2, :] = whole
-            if f == 0:
-                mown[c] = summed
-            else:
-                msend[c, f] = summed.astype(bf16)
-                mtcopy(c, f).start()
-                mcopy(c, f).start()
-        return carry
-
-    def attend_all(c, carry):
-        attend(c)
+            forward(c, f, *merged)
+        return carry
+
+    def bcopy(c, n):
+        part = group(n)
+        return remote(bsend.at[c, part], brecv.at[c, part], bs.at[c, n], br.at[c, n], zdev(-NEAR[n]))
+
+    def btcopy(c, n):
+        part = pl.ds(24 * n, 24) if n < 5 else pl.ds(120, 8)
+        return remote(tb.at[c, part], trb.at[c, part], bts.at[c, n], btr.at[c, n], zdev(-NEAR[n]))
+
+    def ecopy(c, i):
+        return remote(
+            ysend.at[c, yid(Y_OFFS[i])], yrecv.at[c, i], es.at[c, i], er.at[c, i], ydev(Y_OFFS[i])
+        )
+
+    def etcopy(c, i):
+        return remote(yt.at[c, yid(Y_OFFS[i])], ytr.at[c, i], ets.at[c, i], etr.at[c, i], ydev(Y_OFFS[i]))
+
+    def z_first(c, carry):
+        stats = (jnp.zeros((NZ, 128), f32),) * (2 * NY)
+        stats = lax.fori_loop(0, BC, functools.partial(attend_z, c), stats)
+        for i in range(2 * NY):
+            tb[c, pl.ds(i, NZ, stride=8), :] = stats[i]
+
+        def pack(v, carry):
+            for p in range(NZ):
+                bsend[c, p, v] = zb[pl.ds(pl.multiple_of(v * 256 + p * 16, 16), 16), :].astype(bf16)
+            return carry
+
+        lax.fori_loop(0, NY, pack, 0)
+        for n in range(5, 0, -1):
+            btcopy(c, n).start()
+            bcopy(c, n).start()
+        return carry
+
+    def z_middle(c, carry):
+        for n in range(1, 6):
+            btcopy(c, n).wait_recv()
+            bcopy(c, n).wait_recv()
+
+        def one(v, carry):
+            for f in range(3):
+                places = [place(f, n) for n in range(1, SIZE[f])]
+                top, whole, summed = merge_rows(
+                    [tb[c, pl.ds(f * 8 + v * 2 + m, 1), :] for m in range(2)],
+                    [[trb[c, pl.ds(p * 8 + v * 2 + m, 1), :] for m in range(2)] for p in places],
+                    [bsend[c, f, v]] + [brecv[c, p, v] for p in places],
+                )
+                ysend[c, v, f] = summed.astype(bf16)
+                yt[c, v, f * 2 : f * 2 + 1, :] = top
+                yt[c, v, f * 2 + 1 : f * 2 + 2, :] = whole
+            return carry
+
+        lax.fori_loop(0, NY, one, 0)
+        for i in range(3):
+            etcopy(c, i).start()
+            ecopy(c, i).start()
+        return carry
+
+    def z_last(c, carry):
+        for i in range(3):
+            etcopy(c, i).wait_recv()
+            ecopy(c, i).wait_recv()
+        for f in (1, 2, 0):
+            merged = merge_rows(
+                [yt[c, y, f * 2 + m : f * 2 + m + 1, :] for m in range(2)],
+                [[ytr[c, i, f * 2 + m : f * 2 + m + 1, :] for m in range(2)] for i in range(3)],
+                [ysend[c, y, f]] + [yrecv[c, i, f] for i in range(3)],
+            )
+            forward(c, f, *merged)
+        return carry
+
+    def y_first(c, carry):
+        lax.fori_loop(0, BC, functools.partial(attend_y, c), 0)
         pass_on(c)
         return carry
 
-    lax.fori_loop(0, NC, attend_all, 0)
-    lax.fori_loop(0, NC, combine, 0)
-    lax.fori_loop(0, NC, middle, 0)
+    lax.fori_loop(0, NB, z_first, 0)
+    lax.fori_loop(NB, NC, y_first, 0)
+    lax.fori_loop(0, NB, z_middle, 0)
+    lax.fori_loop(NB, NC, combine, 0)
+    lax.fori_loop(0, NB, z_last, 0)
+    lax.fori_loop(NB, NC, middle, 0)
 
     load(8).wait()
     odd16 = lax.rem(lax.broadcasted_iota(jnp.int32, (ROWS, DV), 0), 2) == 1
@@ -346,22 +463,39 @@
             far(f).wait_send()
         for n in range(1, SIZE[f]):
             near(f, n).wait_send()
-        for i in range(2):
-            ycopy(f, i).wait_send()
-            hand(f, i).wait_send()
-
-    def drain(c, carry):
-        for i in range(3):
-            pcopy(c, i).wait_send()
+    for p in range(len(PIECES)):
+        for i in partners(p):
+            ycopy(p, i).wait_send()
+    for i in range(2):
+        hand(i).wait_send()
+
+    def drain_y(c, carry):
+        for i in range(3):
+            for r in range(BC):
+                pcopy(c, r, i).wait_send()
             scopy(c, i).wait_send()
         for n in range(1, 6):
             tcopy(c, n).wait_send()
             ocopy(c, n).wait_send()
+        return carry
+
+    def drain_z(c, carry):
+        for n in range(1, 6):
+            btcopy(c, n).wait_send()
+            bcopy(c, n).wait_send()
+        for i in range(3):
+            etcopy(c, i).wait_send()
+            ecopy(c, i).wait_send()
+        return carry
+
+    def drain(c, carry):
         for f in (1, 2):
             mtcopy(c, f).wait_send()
             mcopy(c, f).wait_send()
         return carry
 
+    lax.fori_loop(0, NB, drain_z, 0)
+    lax.fori_loop(NB, NC, drain_y, 0)
     lax.fori_loop(0, NC, drain, 0)
 
 
@@ -402,17 +536,30 @@
             vmem((NC, 3, 16, PART), bf16),
             vmem((NC, 3, 2, 128), f32),
             vmem((NC, 3, 2, 128), f32),
+            vmem((NY * NZ * 16, PART), f32),
+            vmem((NB, NZ, NY, 16, PART), bf16),
+            vmem((NB, NZ, NY, 16, PART), bf16),
+            vmem((NB, NZ * 8, 128), f32),
+            vmem((NB, NZ * 8, 128), f32),
+            vmem((NB, NY, 3, 16, PART), bf16),
+            vmem((NB, 3, 3, 16, PART), bf16),
+            vmem((NB, NY, 8, 128), f32),
+            vmem((NB, 3, 8, 128), f32),
             dma((9,)),
             dma((3,)), dma((3,)),
             dma((NZ,)), dma((NZ,)),
-            dma((3, 2)), dma((3, 2)),
-            dma((3, 2)), dma((3, 2)),
-            dma((NC, 3)), dma((NC, 3)),
+            dma((len(PIECES), 3)), dma((len(PIECES), 3)),
+            dma((2,)), dma((2,)),
+            dma((NC, BC, 3)), dma((NC, BC, 3)),
             dma((NC, 3)), dma((NC, 3)),
             dma((NC, 6)), dma((NC, 6)),
             dma((NC, 6)), dma((NC, 6)),
             dma((NC, 3)), dma((NC, 3)),
             dma((NC, 3)), dma((NC, 3)),
+            dma((NB, 6)), dma((NB, 6)),
+            dma((NB, 6)), dma((NB, 6)),
+            dma((NB, 3)), dma((NB, 3)),
+            dma((NB, 3)), dma((NB, 3)),
         ],
         compiler_params=pltpu.CompilerParams(
             collective_id=0, has_side_effects=True, vmem_limit_bytes=60 * 1024 * 1024

time: 61.3 us -> 60.4 us (0.985)
  Pallas kernels: 59.8 us -> 58.9 us
    pallas_call x1, Pallas kernels: 59.8 us -> 58.9 us  [per_device(): pl.pallas_call(kernel, out_shape=jax.ShapeDtypeStruct((ROWS, DV), bf16),...]
where the time goes in v4:
time: 60.4 us; the launch traced here: 60.2 us
  Pallas kernels  58.9 us (98%)
  local copies, waits for them, and re-layouts  1.28 us (2%)
    pallas_call x1, Pallas kernels, per_device(): pl.pallas_call(kernel, out_shape=jax.ShapeDtypeStruct((ROWS, DV), bf16),...  58.9 us
    unnamed x1, local copies, waits for them, and re-layouts  1.28 us

profile of v4, /device:TPU:4, one launch (start us, length us, event | category | flops | bytes accessed | tf_op | source)
XLA Modules:
  0.0 60.2 jit_solution(7716242984271380358)
XLA Ops:
  0.0 58.9 %latent_decode.1 = bf16[16,128]{1,0:T(8,128)(2,1)} custom-call(bf16[16,128]{1,0:T(8,128)(2,1)} %bitcast.7, bf16[16,64]{1,0:T(8,128)(2,1)} %bitcast.8, bf16[2,128,512]{2,1,0:T(8,128)(2,1)} %wk_hbm.1, bf16[2,512,128]{2,1,0:T(8,128)(2,1)} %wv_hbm.1, bf16[8,384,512]{2,1,0:T(8,128)(2,1)} %codes_hbm.1, bf16[8,64,384]{2,1,0:T(8,128)(2,1)} %bitcast.5, ...), custom_call_target="tpu_custom_call" | custom-call | flops 860000000 | bytes 4500000 | tf_op jit(solution)/shard_map/latent_decode/pallas_call | solution.py:508
  58.9 1.3 %copy.11 = bf16[8,2,128]{2,1,0:T(2,128)(2,1)} copy(bf16[8,2,128]{2,1,0:T(2,128)(2,1)} %bitcast.6) | data formatting | bytes 8192

commit v5 on v4

--- a/solution.py
+++ b/solution.py
@@ -23,8 +23,8 @@
 NEAR = (0, 1, -1, 2, -2, 3)
 SIZE = (5, 6, 5)
 FIRST = (0, 5, 11)
-PIECES = ((0, 1), (1, 4), (5, 1), (6, 5), (11, 1), (12, 4))
-HANDED = 3
+PIECES = ((0, 5), (5, 6), (11, 5))
+HANDED = 1
 Z_PARTNERS = (5, -5, 3, -3, 2, -2, 1, -1)
 
 
@@ -153,28 +153,24 @@
     far(1).start()
     far(2).start()
     near_start(0)
+    near_wait(0)
     y_start(0)
-    near_wait(0)
-    y_start(1)
     far(1).wait_recv()
     near_start(1)
-    y_start(2)
     far(2).wait_recv()
     near_start(2)
-    y_start(4)
     near_wait(1)
-    y_start(3)
+    y_start(1)
     near_wait(2)
-    y_start(5)
-    for p in (0, 1, 2, 4):
-        widen(p)
+    y_start(2)
+    widen(0)
     for i in range(2):
         ycopy(HANDED, i).wait_recv()
         hand(i).start()
     for i in range(3, 8):
         load(i).wait()
-    widen(5)
-    widen(3)
+    widen(2)
+    widen(1)
 
     def pcopy(c, r, i):
         return remote(

time: 60.4 us -> 59.6 us (0.987)
  the two profiles are of different devices: /device:TPU:4 before, /device:TPU:2 now
where the time goes in v5:
time: 59.6 us; the launch traced here: 59.4 us
  Pallas kernels  58.2 us (98%)
  local copies, waits for them, and re-layouts  1.28 us (2%)
    pallas_call x1, Pallas kernels, per_device(): pl.pallas_call(kernel, out_shape=jax.ShapeDtypeStruct((ROWS, DV), bf16),...  58.2 us
    unnamed x1, local copies, waits for them, and re-layouts  1.28 us

profile of v5, /device:TPU:2, one launch (start us, length us, event | category | flops | bytes accessed | tf_op | source)
XLA Modules:
  0.0 59.4 jit_solution(10494995935988442000)
XLA Ops:
  0.0 58.2 %latent_decode.1 = bf16[16,128]{1,0:T(8,128)(2,1)} custom-call(bf16[16,128]{1,0:T(8,128)(2,1)} %bitcast.7, bf16[16,64]{1,0:T(8,128)(2,1)} %bitcast.8, bf16[2,128,512]{2,1,0:T(8,128)(2,1)} %wk_hbm.1, bf16[2,512,128]{2,1,0:T(8,128)(2,1)} %wv_hbm.1, bf16[8,384,512]{2,1,0:T(8,128)(2,1)} %codes_hbm.1, bf16[8,64,384]{2,1,0:T(8,128)(2,1)} %bitcast.5, ...), custom_call_target="tpu_custom_call" | custom-call | flops 860000000 | bytes 4500000 | tf_op jit(solution)/shard_map/latent_decode/pallas_call | solution.py:504
  58.2 1.3 %copy.11 = bf16[8,2,128]{2,1,0:T(2,128)(2,1)} copy(bf16[8,2,128]{2,1,0:T(2,128)(2,1)} %bitcast.6) | data formatting | bytes 8192

commit v6 on v5

--- a/solution.py
+++ b/solution.py
@@ -75,7 +75,7 @@
     def load(i):
         return pltpu.make_async_copy(pairs[i][0], pairs[i][1], load_sem.at[i])
 
-    for i in range(len(pairs)):
+    for i in range(3):
         load(i).start()
 
     barrier = pltpu.get_barrier_semaphore()
@@ -83,6 +83,9 @@
         pl.semaphore_signal(barrier, inc=1, device_id=zdev(k), device_id_type=MESH)
     for k in Y_OFFS:
         pl.semaphore_signal(barrier, inc=1, device_id=ydev(k), device_id_type=MESH)
+
+    for i in range(3, len(pairs)):
+        load(i).start()
 
     for i in range(3):
         load(i).wait()

time: 59.6 us -> 59.6 us (level)
  no operation moved by 1% of the time
where the time goes in v6:
time: 59.6 us; the launch traced here: 59.4 us
  Pallas kernels  58.2 us (98%)
  local copies, waits for them, and re-layouts  1.28 us (2%)
    pallas_call x1, Pallas kernels, per_device(): pl.pallas_call(kernel, out_shape=jax.ShapeDtypeStruct((ROWS, DV), bf16),...  58.2 us
    unnamed x1, local copies, waits for them, and re-layouts  1.28 us

profile of v6, /device:TPU:2, one launch (start us, length us, event | category | flops | bytes accessed | tf_op | source)
XLA Modules:
  0.0 59.4 jit_solution(14307623279166439744)
XLA Ops:
  0.0 58.2 %latent_decode.1 = bf16[16,128]{1,0:T(8,128)(2,1)} custom-call(bf16[16,128]{1,0:T(8,128)(2,1)} %bitcast.7, bf16[16,64]{1,0:T(8,128)(2,1)} %bitcast.8, bf16[2,128,512]{2,1,0:T(8,128)(2,1)} %wk_hbm.1, bf16[2,512,128]{2,1,0:T(8,128)(2,1)} %wv_hbm.1, bf16[8,384,512]{2,1,0:T(8,128)(2,1)} %codes_hbm.1, bf16[8,64,384]{2,1,0:T(8,128)(2,1)} %bitcast.5, ...), custom_call_target="tpu_custom_call" | custom-call | flops 860000000 | bytes 4500000 | tf_op jit(solution)/shard_map/latent_decode/pallas_call | solution.py:507
  58.2 1.3 %copy.11 = bf16[8,2,128]{2,1,0:T(2,128)(2,1)} copy(bf16[8,2,128]{2,1,0:T(2,128)(2,1)} %bitcast.6) | data formatting | bytes 8192
